TPU v7x, 32 devices: a whole 2x2x4 slice. The times are simulated.
32 devices in a mesh: tm: 8 (over z, x), space: 4 (over y, core).
Axes of the slice: x: 2, y: 2, z: 4, core: 2. Of those that a mesh axis runs over, the one named last changes fastest.
Arguments:
- latent: bfloat16 [2, 8, 512, 1152], P(None, 'tm', 'space'), may hold values from -6 to 6
- spatial_cache: bfloat16 [2, 8, 512, 1152], P(None, 'tm', 'space'), may hold values from -6 to 6
- modulation: float32 [2, 2, 3, 1152], replicated, may hold values from -3 to 3
- weights: bfloat16 [2, 1152, 4608], P(None, 'tm'), may hold values from -0.1875 to 0.1875
Outputs:
- block_out: bfloat16 [2, 8, 512, 1152], P(None, 'tm', 'space')
- new_spatial: bfloat16 [2, 8, 512, 1152], P(None, 'tm', 'space')
- new_temporal: bfloat16 [2, 8, 512, 1152], P(None, 'tm', 'space')
All inputs are finite; a program needn't handle non-finite values.
Results may differ from a plain program's by a relative error of at most 0.015.
Values may be sent and summed in bfloat16 or wider, within the bound.
A program may use at most 128 MiB of HBM per device.

v0:
```python
import jax
import jax.numpy as jnp
from jax import lax
from jax.sharding import PartitionSpec as P

D = 1152
HEAD_DIM = 72


def layer_norm(h):
    x = h.astype(jnp.float32)
    mean = jnp.mean(x, axis=-1, keepdims=True)
    var = jnp.mean((x - mean) ** 2, axis=-1, keepdims=True)
    return (x - mean) * lax.rsqrt(var + 1e-06)


def modulate(h, mods):
    return (layer_norm(h) * (1.0 + mods[1]) + mods[0]).astype(jnp.bfloat16)


def rms_norm(v):
    return v * lax.rsqrt(jnp.mean(v * v, axis=-1, keepdims=True) + 1e-06)


def pack_heads(qkv):
    lead = qkv.shape[:-1]
    split = qkv.reshape(lead + (qkv.shape[-1] // (3 * HEAD_DIM), 3, HEAD_DIM))
    normed = jnp.stack(
        [rms_norm(split[..., 0, :]), rms_norm(split[..., 1, :]), split[..., 2, :]], axis=-2
    )
    return normed.astype(jnp.bfloat16).reshape(qkv.shape)


def attend(packed):
    count, length, width = packed.shape
    heads_here = width // (3 * HEAD_DIM)
    split = packed.reshape(count, length, heads_here, 3, HEAD_DIM)
    scores = jnp.einsum(
        "nlhd,nmhd->nhlm", split[..., 0, :], split[..., 1, :], preferred_element_type=jnp.float32
    )
    expo = jnp.exp(scores / jnp.sqrt(jnp.float32(HEAD_DIM)))
    probs = (expo / jnp.sum(expo, axis=-1, keepdims=True)).astype(jnp.bfloat16)
    out = jnp.einsum("nhlm,nmhd->nlhd", probs, split[..., 2, :], preferred_element_type=jnp.float32)
    return out.astype(jnp.bfloat16).reshape(count, length, heads_here * HEAD_DIM)


def spatial_attend(packed):
    out = lax.map(attend, packed)
    return out


def temporal_attend(packed):
    batch, frames, tokens, width = packed.shape
    tokens_major = jnp.transpose(packed, (0, 2, 1, 3)).reshape(batch * tokens, frames, width)
    out = attend(tokens_major)
    return jnp.transpose(out.reshape(batch, tokens, frames, out.shape[-1]), (0, 2, 1, 3))


def fetch_weight(shard):
    return lax.all_gather(shard, "tm", axis=0, tiled=True)


def project_out(attn, weight):
    shape = attn.shape
    proj = jnp.dot(
        attn.reshape(-1, shape[-1]), weight[:, 3 * D :], preferred_element_type=jnp.float32
    )
    return proj.astype(jnp.bfloat16).reshape(shape)


def project_all(modin, weight):
    shape = modin.shape
    qkv = jnp.dot(
        modin.reshape(-1, shape[-1]), weight[:, : 3 * D], preferred_element_type=jnp.float32
    )
    return pack_heads(qkv).reshape(shape[:-1] + (3 * D,))


def add_gated(h, gate, branch):
    return (h.astype(jnp.float32) + gate * branch.astype(jnp.float32)).astype(jnp.bfloat16)


def shards(latent, spatial_cache, modulation, weights):
    h = add_gated(latent, modulation[0, 0, 2], spatial_cache)
    temporal_weight = fetch_weight(weights[1])
    packed = project_all(modulate(h, modulation[0, 1]), temporal_weight)
    attn = temporal_attend(lax.all_to_all(packed, "tm", split_axis=2, concat_axis=1, tiled=True))
    attn = lax.all_to_all(attn, "tm", split_axis=1, concat_axis=2, tiled=True)
    new_temporal = project_out(attn, temporal_weight)
    h = add_gated(h, modulation[0, 1, 2], new_temporal)
    spatial_weight = fetch_weight(weights[0])
    modin = modulate(h, modulation[1, 0])
    packed = project_all(modin, spatial_weight)
    attn = spatial_attend(lax.all_to_all(packed, "space", split_axis=3, concat_axis=2, tiled=True))
    attn = lax.all_to_all(attn, "space", split_axis=2, concat_axis=3, tiled=True)
    new_spatial = project_out(attn, spatial_weight)
    h = add_gated(h, modulation[1, 0, 2], new_spatial)
    block_out = add_gated(h, modulation[1, 1, 2], new_temporal)
    return (block_out, new_spatial, new_temporal)


def solution(mesh):
    in_specs = (
        P(None, "tm", "space", None),
        P(None, "tm", "space", None),
        P(),
        P(None, "tm", None),
    )
    out_specs = (
        P(None, "tm", "space", None),
        P(None, "tm", "space", None),
        P(None, "tm", "space", None),
    )
    return jax.shard_map(shards, mesh=mesh, in_specs=in_specs, out_specs=out_specs, check_vma=False)
```

profile of v0, /device:TPU:1, one launch (start us, length us, event | category | flops | bytes accessed | tf_op | source)
XLA Modules:
  0.0 449.4 jit_solution(5322218657583536191)
XLA Ops:
  7.2 3.5 fusion.40
  10.7 0.7 all-gather.7.cloned.1.call-update
  11.9 0.3 convert_reduce_fusion.1
  12.2 0.3 fusion.25
  12.6 0.3 fusion.28
  12.9 152.1 %all-gather.5.cloned.1.call-done = bf16[1,1152,4608]{2,1,0:T(8,128)(2,1)} async-done(((bf16[1,144,4608]{2,1,0:T(8,128)(2,1)}), bf16[1,1152,4608]{2,1,0:T(8,128)(2,1)}) %all-gather.5.cloned.1.call-update) | async-done | bytes 10616848 | tf_op jit(solution)/shard_map/all_gather | solution.py:60
  165.0 6.9 %slice_bitcast_fusion.7 = bf16[3456,1152]{0,1:T(8,128)(2,1)} fusion(bf16[1152,4608]{1,0:T(8,128)(2,1)} %bitcast.124), kind=kLoop, calls=%fused_computation.13 | loop fusion | bytes 15925248 | tf_op jit(solution)/shard_map/dot_general | solution.py:73
  171.9 11.7 %copy.89 = bf16[3456,1152]{1,0:T(8,128)(2,1)} copy(bf16[3456,1152]{0,1:T(8,128)(2,1)} %slice_bitcast_fusion.7) | data formatting | bytes 15925248 | tf_op jit(solution)/shard_map/dot_general | solution.py:73
  183.6 5.8 %fusion.41 = f32[256,16,3,72]{0,3,2,1:T(8,128)S(1)} fusion(bf16[256,1152,1,1]{1,0,3,2:T(8,128)(2,1)S(1)} %bitcast.131, bf16[16,3,72,1152]{3,2,1,0:T(8,128)(2,1)} %bitcast.117), kind=kOutput, calls=%fused_computation.88 | convolution fusion | flops 2038431744 | bytes 12091392 | tf_op jit(solution)/shard_map/dot_general | solution.py:73
  189.7 0.2 multiply_convert_fusion.3
  190.2 1.9 convert_element_type.117
  192.1 5.9 %copy.90 = bf16[2,1,128,3456]{3,0,1,2:T(2,128)(2,1)S(1)} copy(bf16[2,1,128,3456]{2,0,3,1:T(2,128)(2,1)} %convert_element_type.117) | data formatting | bytes 3538944 | tf_op jit(solution)/shard_map/convert_element_type | solution.py:31
  198.0 72.5 %all_to_all.54 = bf16[2,1,128,3456]{3,0,1,2:T(2,128)(2,1)S(1)} all-to-all(bf16[2,1,128,3456]{3,0,1,2:T(2,128)(2,1)S(1)} %copy.90), channel_id=1, replica_groups=mesh['tm'=8,'space'=4] {'tm'}, dimensions={2} | all-to-all | bytes 3538944 | tf_op jit(solution)/shard_map/all_to_all | solution.py:87
  270.7 0.3 copy.92
  271.0 7.4 %reshape_reshape.8 = bf16[32,8,16,3,72]{4,3,2,1,0:T(4,128)(2,1)} reshape(bf16[2,16,8,3456]{3,2,1,0:T(8,128)(2,1)S(1)} %copy.92) | data formatting | bytes 3538944 | tf_op jit(solution)/shard_map/reshape;reshape | solution.py:37
  278.4 11.0 %fusion.39 = (bf16[32,8,16,1,72]{4,3,2,1,0:T(2,128)(2,1)S(1)}, bf16[32,8,16,1,72]{4,3,2,1,0:T(2,128)(2,1)S(1)}, bf16[32,8,16,1,72]{4,3,2,1,0:T(2,128)(2,1)S(1)}) fusion(bf16[32,8,16,3,72]{4,3,2,1,0:T(4,128)(2,1)} %reshape_reshape.8), kind=kLoop, calls=%fused_computation.86 | loop fusion | bytes 3538944 | tf_op jit(solution)/shard_map/slice | solution.py:39
  289.5 1.8 fusion.15
  291.3 1.1 fusion.20
  292.4 0.2 copy.97
  292.6 1.3 reshape_reshape.9
  293.9 0.9 copy.98
  294.8 3.8 all-to-all-start.1
  298.6 60.3 %all-gather.7.cloned.1.call-done = bf16[1,1152,4608]{2,1,0:T(8,128)(2,1)} async-done(((bf16[1,144,4608]{2,1,0:T(8,128)(2,1)}), bf16[1,1152,4608]{2,1,0:T(8,128)(2,1)}) %all-gather.7.cloned.1.call-update) | async-done | bytes 10616848 | tf_op jit(solution)/shard_map/all_gather | solution.py:60
  358.9 6.9 %slice_bitcast_fusion.6 = bf16[3456,1152]{0,1:T(8,128)(2,1)} fusion(bf16[1152,4608]{1,0:T(8,128)(2,1)} %bitcast.122), kind=kLoop, calls=%fused_computation.12 | loop fusion | bytes 15925248 | tf_op jit(solution)/shard_map/dot_general | solution.py:73
  365.9 11.5 %copy.101 = bf16[3456,1152]{1,0:T(8,128)(2,1)} copy(bf16[3456,1152]{0,1:T(8,128)(2,1)} %slice_bitcast_fusion.6) | data formatting | bytes 15925248 | tf_op jit(solution)/shard_map/dot_general | solution.py:73
  377.4 2.9 fusion.9
  380.3 0.3 convert_reduce_fusion
  380.6 0.3 fusion.21
  380.9 0.3 fusion.24
  381.2 0.4 copy-done
  381.7 2.6 fusion.42
  384.6 0.2 multiply_convert_fusion.1
  385.0 1.9 convert_element_type.126
  386.9 4.0 all-to-all-start.2
  390.9 21.3 %all-to-all-done.2 = bf16[2,1,128,3456]{2,0,1,3:T(2,128)(2,1)S(1)} async-done(((bf16[2,1,128,3456]{2,0,1,3:T(2,128)(2,1)}), bf16[2,1,128,3456]{2,0,1,3:T(2,128)(2,1)S(1)}, u32[]{:S(2)}, u32[]{:S(2)}) %all-to-all-start.2) | async-done | bytes 1769504 | tf_op jit(solution)/shard_map/all_to_all | solution.py:94
  412.3 2.6 copy.103
  414.8 3.0 all_to_all.46
  417.9 3.6 while.10
  417.9 0.8 fusion.50
  418.8 0.8 fusion.51
  419.8 0.8 fusion.50
  420.6 0.8 fusion.51
  421.5 1.2 copy.104
  422.7 13.9 %all_to_all.55 = bf16[2,1,512,288]{3,0,1,2:T(2,128)(2,1)S(1)} all-to-all(bf16[2,1,512,288]{3,0,1,2:T(2,128)(2,1)S(1)} %copy.104), channel_id=1, replica_groups=mesh['tm'=8,'space'=4] {'space'}, dimensions={2} | all-to-all | bytes 1179648 | tf_op jit(solution)/shard_map/all_to_all | solution.py:95
  436.6 1.4 copy.114
  438.0 0.6 copy.106
  438.6 2.8 fusion.12
  441.4 1.1 fusion.30
  (36 shorter events, 2.0 us)
Async XLA Ops:
  7.2 157.8 %all-gather.5.cloned.1.call-start = ((), (), s32[]{:S(2)}) async-start(), calls=%async_computation.4 | async-start | bytes 11943936 | tf_op jit(solution)/shard_map/all_gather | solution.py:60
  10.7 0.8 copy-start.5
  10.7 1.1 copy-start.2
  10.7 1.3 copy-start.3
  10.7 348.2 %all-gather.7.cloned.1.call-start = ((), (), s32[]{:S(2)}) async-start(), calls=%async_computation.5 | async-start | bytes 11943936 | tf_op jit(solution)/shard_map/all_gather | solution.py:60
  294.8 82.5 %all-to-all-start.1 = ((bf16[2,8,16,1152]{3,2,0,1:T(8,128)(2,1)}), bf16[2,8,16,1152]{3,2,0,1:T(8,128)(2,1)S(1)}, u32[]{:S(2)}, u32[]{:S(2)}) async-start(bf16[2,8,16,1152]{3,2,0,1:T(8,128)(2,1)} %copy.98), calls=%async_computation.1 | async-start | bytes 1179648 | tf_op jit(solution)/shard_map/all_to_all | solution.py:88
  377.4 4.3 copy-start
  380.3 61.1 %copy-start.1 = (bf16[256,1152]{1,0:T(8,128)(2,1)}, bf16[256,1152]{1,0:T(8,128)(2,1)S(1)}, u32[]{:S(2)}) copy-start(bf16[256,1152]{1,0:T(8,128)(2,1)S(1)} %fusion.9) | copy-start | bytes 1769476
  386.9 25.3 %all-to-all-start.2 = ((bf16[2,1,128,3456]{2,0,1,3:T(2,128)(2,1)}), bf16[2,1,128,3456]{2,0,1,3:T(2,128)(2,1)S(1)}, u32[]{:S(2)}, u32[]{:S(2)}) async-start(bf16[2,1,128,3456]{2,0,1,3:T(2,128)(2,1)} %bitcast.120), calls=%async_computation.2 | async-start | bytes 3538944 | tf_op jit(solution)/shard_map/all_to_all | solution.py:94
  441.4 1.1 copy-start.4
Sparse Core Ops, SparseCore 0:
  10.8 154.1 all-gather.4
  167.1 191.7 all-gather.6
where the time goes:
time: 452 us; the launch traced here: 449 us
  waiting for transfers between devices  234 us (52%)
  blocking collectives  86.4 us (19%)
  local copies, waits for them, and re-layouts  81.5 us (18%)
  matrix products  20.4 us (5%)
  between operations  14.3 us (3%)
  starting transfers between devices  7.84 us (2%)
    all_gather x2, waiting for transfers between devices, fetch_weight(): return lax.all_gather(shard, 'tm', axis=0, tiled=True)  212 us
    all_to_all x1, blocking collectives, shards(): lax.all_to_all(packed, 'tm', split_axis=2, concat_axis=1, tiled=True)  72.5 us
    dot_general x4, local copies, waits for them, and re-layouts, project_all(): jnp.dot(modin.reshape(-1, shape[-1]), weight[:, :3 * D], preferred_elemen...  37 us
    all_to_all x1, waiting for transfers between devices, shards(): lax.all_to_all(packed, 'space', split_axis=3, concat_axis=2, tiled=True)  21.3 us
    all_to_all x1, blocking collectives, shards(): lax.all_to_all(attn, 'space', split_axis=2, concat_axis=3, tiled=True)  13.9 us
    slice x1, local copies, waits for them, and re-layouts, attend(): split[..., 0, :]  11 us
    convert_element_type x3, local copies, waits for them, and re-layouts, pack_heads(): return normed.astype(jnp.bfloat16).reshape(qkv.shape)  9.76 us
  transfers between devices with their start and end apart: 4, of which 3 were waited for; matrix products, arithmetic and copies ran while one was open for 17% of the time, Pallas kernels for 0%

commit v1 on v0

v1 whole, which is shorter than its diff:
```python
import functools

import jax
import jax.numpy as jnp
from jax import lax
from jax.experimental import pallas as pl
from jax.experimental.pallas import tpu as pltpu
from jax.sharding import PartitionSpec as P

D = 1152
HEADS = 16
HEAD_DIM = 72
MESH = pl.DeviceIdType.MESH
VMEM = pltpu.VMEM
LIMIT = 56 * 1024 * 1024


def add_gated(h, gate, branch):
    return (h.astype(jnp.float32) + gate * branch.astype(jnp.float32)).astype(jnp.bfloat16)


def modulate(h, shift, scale):
    x = h.astype(jnp.float32)
    mean = jnp.mean(x, axis=-1, keepdims=True)
    c = x - mean
    var = jnp.mean(c * c, axis=-1, keepdims=True)
    return (c * lax.rsqrt(var + 1e-06) * (1.0 + scale) + shift).astype(jnp.bfloat16)


def mod_row(mod_ref, step, attn, which):
    row = (step * 2 + attn) * 3 + which
    return mod_ref[row : row + 1, :]


def place():
    return lax.axis_index("tm"), lax.axis_index("space")


def device(t, s):
    return {"tm": t, "space": s}


def greet(peers):
    barrier = pltpu.get_barrier_semaphore()
    for t, s in peers:
        pl.semaphore_signal(barrier, inc=1, device_id=device(t, s), device_id_type=MESH)
    pl.semaphore_wait(barrier, len(peers))


def tm_peers(nt, t, s):
    return [(lax.rem(t + k, nt), s) for k in range(1, nt)]


def space_peers(ns, t, s):
    return [(t, lax.rem(s + k, ns)) for k in range(1, ns)]


def chip_peers(ns, s):
    return [lax.rem(s + 2 * k, ns) for k in range(1, ns // 2)], s + 1 - 2 * lax.rem(s, 2)


def remote(src, dst, send, recv, t, s):
    return pltpu.make_async_remote_copy(
        src_ref=src, dst_ref=dst, send_sem=send, recv_sem=recv, device_id=device(t, s), device_id_type=MESH
    )


def spread(slots, send, recv, ns, t, s, chunks, ready):
    others, sib = chip_peers(ns, s)
    started = []
    for n, i in enumerate(chunks):
        ready(i)
        for k, o in enumerate(others):
            c = remote(slots.at[s, i], slots.at[s, i], send.at[k, n], recv.at[s, i], t, o)
            c.start()
            started.append(c)
        c = remote(slots.at[s, i], slots.at[s, i], send.at[len(others), n], recv.at[s, i], t, sib)
        c.start()
        started.append(c)
    for n, i in enumerate(chunks):
        for k, o in enumerate(others):
            got = remote(slots.at[o, i], slots.at[o, i], send.at[0, 0], recv.at[o, i], t, sib)
            got.wait_recv()
            c = remote(slots.at[o, i], slots.at[o, i], send.at[len(others) + 1 + k, n], recv.at[o, i], t, sib)
            c.start()
            started.append(c)
    for n, i in enumerate(chunks):
        for base in [sib] + [o + sib - s for o in others]:
            remote(slots.at[base, i], slots.at[base, i], send.at[0, 0], recv.at[base, i], t, sib).wait_recv()
    return started


def enter_kernel(nt, ns, lat, cache, mod, x, h_out, own, send_a, send_b, recv):
    t, s = place()
    greet(tm_peers(nt, t, s) + space_peers(ns, t, s))
    h = add_gated(lat[...], mod_row(mod, 0, 0, 2), cache[...])
    h_out[...] = h
    own[...] = modulate(h, mod_row(mod, 0, 1, 0), mod_row(mod, 0, 1, 1)).reshape(own.shape)
    started = []
    for k in range(1, nt):
        p = lax.rem(t + k, nt)
        c = remote(own.at[p], x.at[s, t], send_a.at[k], recv.at[s, t], p, s)
        c.start()
        started.append(c)
    x[s, t] = own[t]

    order = [t] + [lax.rem(t + nt - k, nt) for k in range(1, nt)]

    def ready(q):
        if q is not t:
            remote(own.at[0], x.at[s, q], send_a.at[0], recv.at[s, q], t, s).wait_recv()

    started += spread(x, send_b, recv, ns, t, s, order, ready)
    for c in started:
        c.wait_send()


def heads_of(qkv, heads):
    out = []
    for i in range(heads):
        parts = [qkv[:, (3 * i + j) * HEAD_DIM : (3 * i + j + 1) * HEAD_DIM] for j in range(3)]
        for j in range(2):
            sq = jnp.sum(parts[j] * parts[j], axis=-1, keepdims=True)
            parts[j] = parts[j] * lax.rsqrt(sq * (1.0 / HEAD_DIM) + 1e-06)
        out.append([p.astype(jnp.bfloat16) for p in parts])
    return out


def attend(q, k, v, mask):
    scores = lax.dot_general(q, k, (((1,), (1,)), ((), ())), preferred_element_type=jnp.float32)
    expo = jnp.exp(scores * (HEAD_DIM**-0.5))
    if mask is not None:
        expo = jnp.where(mask, expo, 0.0)
    probs = (expo / jnp.sum(expo, axis=-1, keepdims=True)).astype(jnp.bfloat16)
    return jnp.dot(probs, v, preferred_element_type=jnp.float32).astype(jnp.bfloat16)


def project(o, wo, ns):
    acc = jnp.dot(o[0], wo[0], preferred_element_type=jnp.float32)
    for i in range(1, ns):
        acc += jnp.dot(o[i], wo[i], preferred_element_type=jnp.float32)
    return acc.astype(jnp.bfloat16)


def temporal_kernel(
    nt, ns, x, wq, wo, h_ref, mod, x2, h_out, new_t, mine, o, y, back, send_o, recv_o, send_y, recv_y, send_b, recv_b
):
    t, s = place()
    greet(tm_peers(nt, t, s) + space_peers(ns, t, s))
    heads = HEADS // ns
    rows = x.shape[1]
    block = rows // nt
    mask = lax.rem(lax.broadcasted_iota(jnp.int32, (rows, rows), 0), block) == lax.rem(
        lax.broadcasted_iota(jnp.int32, (rows, rows), 1), block
    )

    def tile(step, carry):
        p = lax.rem(s + step, ns)
        qkv = jnp.dot(x[p], wq[...], preferred_element_type=jnp.float32)
        outs = [attend(q, k, v, mask) for q, k, v in heads_of(qkv, heads)]
        mine[p] = jnp.concatenate(outs, axis=-1)

        @pl.when(step < ns)
        def _():
            remote(mine.at[p], o.at[s], send_o.at[step], recv_o.at[s], t, p).start()

        return carry

    lax.fori_loop(1, ns + 1, tile, 0)
    o[s] = mine[s]
    for k in range(1, ns):
        q = lax.rem(s + k, ns)
        remote(mine.at[q], o.at[q], send_o.at[k], recv_o.at[q], t, q).wait_recv()
    y[...] = project(o, wo, ns).reshape(y.shape)
    started = []
    for k in range(1, nt):
        p = lax.rem(t + k, nt)
        c = remote(y.at[p], back.at[t], send_y.at[k], recv_y.at[t], p, s)
        c.start()
        started.append(c)
    back[t] = y[t]
    for k in range(1, nt):
        q = lax.rem(t + k, nt)
        remote(y.at[q], back.at[q], send_y.at[k], recv_y.at[q], q, s).wait_recv()
    fresh = back[...].reshape(rows, D)
    new_t[...] = fresh
    h = add_gated(h_ref[...], mod_row(mod, 0, 1, 2), fresh)
    h_out[...] = h
    x2[s] = modulate(h, mod_row(mod, 1, 0, 0), mod_row(mod, 1, 0, 1)).reshape(x2.shape[1:])
    started += spread(x2, send_b, recv_b, ns, t, s, list(range(x2.shape[1])), lambda i: None)
    for k in range(1, ns):
        q = lax.rem(s + k, ns)
        remote(mine.at[q], o.at[q], send_o.at[k], recv_o.at[q], t, q).wait_send()
    for c in started:
        c.wait_send()


def spatial_kernel(
    batch, ns, x, wq, wo, h_ref, nt_ref, mod, block_out, new_s, qs, ks, vs, mine, o, send_o, recv_o
):
    t, s = place()
    greet(space_peers(ns, t, s))
    heads = HEADS // ns
    rows = x.shape[1]
    span = rows // batch

    def proj(p, carry):
        qkv = jnp.dot(x[p], wq[...], preferred_element_type=jnp.float32)
        for i, (q, k, v) in enumerate(heads_of(qkv, heads)):
            for b in range(batch):
                part = slice(b * span, (b + 1) * span)
                qs[p, i, b] = q[part]
                ks[i, b, p] = k[part]
                vs[i, b, p] = v[part]
        return carry

    lax.fori_loop(0, ns, proj, 0)

    def tile(step, carry):
        p = lax.rem(s + step, ns)
        for b in range(batch):
            outs = []
            for i in range(heads):
                keys = ks[i, b].reshape(ns * span, HEAD_DIM)
                vals = vs[i, b].reshape(ns * span, HEAD_DIM)
                outs.append(attend(qs[p, i, b], keys, vals, None))
            mine[p, b * span : (b + 1) * span, :] = jnp.concatenate(outs, axis=-1)

        @pl.when(step < ns)
        def _():
            remote(mine.at[p], o.at[s], send_o.at[step], recv_o.at[s], t, p).start()

        return carry

    lax.fori_loop(1, ns + 1, tile, 0)
    o[s] = mine[s]
    for k in range(1, ns):
        q = lax.rem(s + k, ns)
        remote(mine.at[q], o.at[q], send_o.at[k], recv_o.at[q], t, q).wait_recv()
    fresh = project(o, wo, ns)
    new_s[...] = fresh
    h = add_gated(h_ref[...], mod_row(mod, 1, 0, 2), fresh)
    block_out[...] = add_gated(h, mod_row(mod, 1, 1, 2), nt_ref[...])
    for k in range(1, ns):
        q = lax.rem(s + k, ns)
        remote(mine.at[q], o.at[q], send_o.at[k], recv_o.at[q], t, q).wait_send()


def call(kernel, args, outs, scratch, collective_id, flops):
    return pl.pallas_call(
        kernel,
        out_shape=[jax.ShapeDtypeStruct(shape, jnp.bfloat16) for shape in outs],
        in_specs=[pl.BlockSpec(memory_space=VMEM)] * len(args),
        out_specs=[pl.BlockSpec(memory_space=VMEM)] * len(outs),
        scratch_shapes=scratch,
        cost_estimate=pl.CostEstimate(flops=flops, bytes_accessed=100_000_000, transcendentals=0),
        compiler_params=pltpu.CompilerParams(
            collective_id=collective_id, has_side_effects=True, vmem_limit_bytes=LIMIT
        ),
    )(*args)


def shards(nt, ns, latent, spatial_cache, modulation, weights):
    s = lax.axis_index("space")
    batch, _, span, _ = latent.shape
    rows = batch * span
    block = rows // nt
    wide = 3 * D // ns
    dma = pltpu.SemaphoreType.DMA
    bf16 = jnp.bfloat16
    chunks = 8

    def fetch(a):
        own = lax.dynamic_slice(weights[a], (0, s * wide), (weights.shape[1], wide))
        wq = lax.all_gather(own, "tm", axis=0, tiled=True)
        wo = lax.all_gather(weights[a][:, 3 * D :], "tm", axis=0, tiled=True)
        return wq, wo.reshape(ns, D // ns, D)

    wq_t, wo_t = fetch(1)
    wq_s, wo_s = fetch(0)
    mod = modulation.reshape(12, D)
    x, h = call(
        functools.partial(enter_kernel, nt, ns),
        (latent.reshape(rows, D), spatial_cache.reshape(rows, D), mod),
        [(ns, nt, block, D), (rows, D)],
        [VMEM((nt, block, D), bf16), dma((nt,)), dma((ns, nt)), dma((ns, nt))],
        0,
        1_000_000,
    )
    x2, h, new_t = call(
        functools.partial(temporal_kernel, nt, ns),
        (x.reshape(ns, rows, D), wq_t, wo_t, h, mod),
        [(ns, chunks, rows // chunks, D), (rows, D), (rows, D)],
        [
            VMEM((ns, rows, D // ns), bf16),
            VMEM((ns, rows, D // ns), bf16),
            VMEM((nt, block, D), bf16),
            VMEM((nt, block, D), bf16),
            dma((ns,)),
            dma((ns,)),
            dma((nt,)),
            dma((nt,)),
            dma((ns, chunks)),
            dma((ns, chunks)),
        ],
        1,
        3_000_000_000,
    )
    heads = HEADS // ns
    block_out, new_s = call(
        functools.partial(spatial_kernel, batch, ns),
        (x2.reshape(ns, rows, D), wq_s, wo_s, h, new_t, mod),
        [(rows, D), (rows, D)],
        [
            VMEM((ns, heads, batch, span, HEAD_DIM), bf16),
            VMEM((heads, batch, ns, span, HEAD_DIM), bf16),
            VMEM((heads, batch, ns, span, HEAD_DIM), bf16),
            VMEM((ns, rows, D // ns), bf16),
            VMEM((ns, rows, D // ns), bf16),
            dma((ns,)),
            dma((ns,)),
        ],
        2,
        3_000_000_000,
    )
    return tuple(a.reshape(latent.shape) for a in (block_out, new_s, new_t))


def solution(mesh):
    part = P(None, "tm", "space", None)
    return jax.shard_map(
        functools.partial(shards, mesh.shape["tm"], mesh.shape["space"]),
        mesh=mesh,
        in_specs=(part, part, P(), P(None, "tm", None)),
        out_specs=(part, part, part),
        check_vma=False,
    )
```

time: 452 us -> 280 us (0.62)
  Pallas kernels: 0 us -> 118 us
  waiting for transfers between devices: 234 us -> 133 us
  blocking collectives: 86.4 us -> 0 us
  local copies, waits for them, and re-layouts: 81.5 us -> 14.2 us
  matrix products: 20.4 us -> 0 us
  starting transfers between devices: 7.84 us -> 0.16 us
    pallas_call x0 -> x3, Pallas kernels: none -> 118 us  [call(): pl.pallas_call(kernel, out_shape=[jax.ShapeDtypeStruct(shape, jnp.bfloat1...]
    all_to_all x2 -> x0, blocking collectives: 86.4 us -> none  [the longest x1 72.5 us: shards(): lax.all_to_all(packed, 'tm', split_axis=2, concat_axis=1, tiled=True)]
    all_gather x2 -> x4, waiting for transfers between devices: 212 us -> 133 us  [the longest x2 111 us: fetch(): wo = lax.all_gather(weights[a][:, 3 * D:], 'tm', axis=0, tiled=True)]
    dot_general x4 -> x0, local copies, waits for them, and re-layouts: 37 us -> none  [project_all(): jnp.dot(modin.reshape(-1, shape[-1]), weight[:, :3 * D], preferred_elemen...]
    all_to_all x2 -> x0, waiting for transfers between devices: 21.3 us -> none  [the longest x1 21.3 us: shards(): lax.all_to_all(packed, 'space', split_axis=3, concat_axis=2, tiled=True)]
    dot_general x10 -> x0, matrix products: 20.4 us -> none  [the longest x2 8.39 us: project_all(): jnp.dot(modin.reshape(-1, shape[-1]), weight[:, :3 * D], preferred_elemen...]
    slice x4 -> x2, local copies, waits for them, and re-layouts: 14.6 us -> 1.5 us  [fetch(): wo = lax.all_gather(weights[a][:, 3 * D:], 'tm', axis=0, tiled=True)]
    convert_element_type x4 -> x0, local copies, waits for them, and re-layouts: 9.98 us -> none  [the longest x3 9.76 us: pack_heads(): return normed.astype(jnp.bfloat16).reshape(qkv.shape)]
  transfers between devices with their start and end apart: 4 -> 4, of which waited for: 3 -> 3; matrix products, arithmetic and copies ran while one was open for 17% -> 1% of each run, Pallas kernels for 0% -> 31%
where the time goes in v1:
time: 280 us
  waiting for transfers between devices  133 us (48%)
  Pallas kernels  118 us (42%)
  local copies, waits for them, and re-layouts  14.2 us (5%)
  between operations  13.8 us (5%)
    pallas_call x3, Pallas kernels, call(): pl.pallas_call(kernel, out_shape=[jax.ShapeDtypeStruct(shape, jnp.bfloat1...  118 us
    all_gather x2, waiting for transfers between devices, fetch(): wo = lax.all_gather(weights[a][:, 3 * D:], 'tm', axis=0, tiled=True)  111 us
    all_gather x2, waiting for transfers between devices, fetch(): wq = lax.all_gather(own, 'tm', axis=0, tiled=True)  22.2 us
  transfers between devices with their start and end apart: 4, of which 3 were waited for; matrix products, arithmetic and copies ran while one was open for 1% of the time, Pallas kernels for 31%

profile of v1, /device:TPU:1, one launch (start us, length us, event | category | flops | bytes accessed | tf_op | source)
XLA Modules:
  0.0 279.9 jit_solution(2987512691700394017)
XLA Ops:
  7.2 0.0 all-gather.11.cloned.1.call-start
  7.2 3.7 %slice_bitcast_fusion = (bf16[144,4608]{1,0:T(8,128)(2,1)S(1)}, bf16[144,4608]{1,0:T(8,128)(2,1)S(1)}, bf16[1,144,4608]{2,1,0:T(8,128)(2,1)}, bf16[1,144,4608]{2,1,0:T(8,128)(2,1)}) fusion(bf16[2,144,4608]{2,1,0:T(8,128)(2,1)} %param.7), kind=kLoop, calls=%fused_computation.2 | loop fusion | bytes 7962624 | tf_op jit(solution)/shard_map/squeeze | solution.py:274
  10.9 0.0 copy-start.1
  10.9 1.8 constant_dynamic-slice_fusion.1
  12.7 0.0 all-gather.11.cloned.1.call-update
  12.7 0.0 all-gather.7.cloned.1.call-start
  12.8 0.8 slice.18
  13.5 0.0 all-gather.7.cloned.1.call-update
  13.6 0.0 all-gather.13.cloned.1.call-start
  13.6 1.8 constant_dynamic-slice_fusion
  15.4 0.0 all-gather.13.cloned.1.call-update
  15.5 0.0 all-gather.9.cloned.1.call-start
  15.5 0.8 slice.19
  16.3 0.0 all-gather.9.cloned.1.call-update
  16.3 0.0 copy-done.1
  16.3 0.7 reshape.40.mod
  17.0 32.6 %shard_map.67 = (bf16[4,8,32,1152]{3,2,1,0:T(8,128)(2,1)}, bf16[256,1152]{1,0:T(8,128)(2,1)}) custom-call(bf16[256,1152]{1,0:T(8,128)(2,1)} %bitcast.21, bf16[256,1152]{1,0:T(8,128)(2,1)} %bitcast.22, f32[12,1152]{1,0:T(8,128)} %reshape.40.mod), custom_call_target="tpu_custom_call" | custom-call | flops 1000000 | bytes 100000000 | tf_op jit(solution)/shard_map/pallas_call | solution.py:250
  49.6 22.1 %all-gather.11.cloned.1.call-done = bf16[1,1152,864]{2,1,0:T(8,128)(2,1)} async-done(((bf16[1,144,864]{2,1,0:T(8,128)(2,1)}), bf16[1,1152,864]{2,1,0:T(8,128)(2,1)}) %all-gather.11.cloned.1.call-update) | async-done | bytes 1990672 | tf_op jit(solution)/shard_map/all_gather | solution.py:275
  71.8 56.1 %all-gather.7.cloned.1.call-done = bf16[1152,1152]{1,0:T(8,128)(2,1)} async-done(((bf16[144,1152]{1,0:T(8,128)(2,1)}), bf16[1152,1152]{1,0:T(8,128)(2,1)}) %all-gather.7.cloned.1.call-update) | async-done | bytes 2654224 | tf_op jit(solution)/shard_map/all_gather | solution.py:276
  127.9 55.1 %shard_map.68 = (bf16[4,8,32,1152]{3,2,1,0:T(8,128)(2,1)}, bf16[256,1152]{1,0:T(8,128)(2,1)}, bf16[256,1152]{1,0:T(8,128)(2,1)}) custom-call(bf16[4,256,1152]{2,1,0:T(8,128)(2,1)} %bitcast.28, bf16[1152,864]{1,0:T(8,128)(2,1)} %bitcast.29, bf16[4,288,1152]{2,1,0:T(8,128)(2,1)} %bitcast.26, bf16[256,1152]{1,0:T(8,128)(2,1)} %get-tuple-element.11.h_ref, ...), custom_call_target="tpu_custom_call" | custom-call | flops 3000000000 | bytes 100000000 | tf_op jit(solution)/shard_map/pallas_call | solution.py:250
  183.0 0.0 all-gather.13.cloned.1.call-done
  183.0 55.1 %all-gather.9.cloned.1.call-done = bf16[1152,1152]{1,0:T(8,128)(2,1)} async-done(((bf16[144,1152]{1,0:T(8,128)(2,1)}), bf16[1152,1152]{1,0:T(8,128)(2,1)}) %all-gather.9.cloned.1.call-update) | async-done | bytes 2654224 | tf_op jit(solution)/shard_map/all_gather | solution.py:276
  238.1 30.5 %shard_map.69 = (bf16[256,1152]{1,0:T(8,128)(2,1)}, bf16[256,1152]{1,0:T(8,128)(2,1)}) custom-call(bf16[4,256,1152]{2,1,0:T(8,128)(2,1)} %bitcast.31, bf16[1152,864]{1,0:T(8,128)(2,1)} %bitcast.30, bf16[4,288,1152]{2,1,0:T(8,128)(2,1)} %bitcast.27, bf16[256,1152]{1,0:T(8,128)(2,1)} %get-tuple-element.13.h_ref, bf16[256,1152]{1,0:T(8,128)(2,1)} %get-tuple-element.14.nt_ref, ...), custom_call_target="tpu_custom_call" | custom-call | flops 3000000000 | bytes 100000000 | tf_op jit(solution)/shard_map/pallas_call | solution.py:250
  268.6 0.0 copy-start
  268.6 2.0 copy.18
  270.6 1.9 copy.19
  272.5 0.0 copy-done
  272.6 0.8 copy.20
  (1 shorter events, 0.0 us)
Async XLA Ops:
  7.2 64.6 %all-gather.11.cloned.1.call-start = ((), (), s32[]{:S(2)}) async-start(), calls=%async_computation.2 | async-start | bytes 2322432 | tf_op jit(solution)/shard_map/all_gather | solution.py:275
  10.9 5.4 %copy-start.1 = (f32[2,2,3,1152]{3,1,2,0:T(2,128)S(1)}, f32[2,2,3,1152]{3,1,2,0:T(2,128)}, u32[]{:S(2)}) copy-start(f32[2,2,3,1152]{3,1,2,0:T(2,128)} %param.6) | copy-start | bytes 165892
  12.7 115.2 %all-gather.7.cloned.1.call-start = ((), (), s32[]{:S(2)}) async-start(), calls=%async_computation | async-start | bytes 2985984 | tf_op jit(solution)/shard_map/all_gather | solution.py:276
  13.6 169.4 %all-gather.13.cloned.1.call-start = ((), (), s32[]{:S(2)}) async-start(), calls=%async_computation.3 | async-start | bytes 2322432 | tf_op jit(solution)/shard_map/all_gather | solution.py:275
  15.5 222.6 %all-gather.9.cloned.1.call-start = ((), (), s32[]{:S(2)}) async-start(), calls=%async_computation.1 | async-start | bytes 2985984 | tf_op jit(solution)/shard_map/all_gather | solution.py:276
  268.6 3.9 %copy-start = (bf16[256,1152]{1,0:T(8,128)(2,1)S(1)}, bf16[256,1152]{1,0:T(8,128)(2,1)}, u32[]{:S(2)}) copy-start(bf16[256,1152]{1,0:T(8,128)(2,1)} %get-tuple-element.14.nt_ref) | copy-start | bytes 1769476
Sparse Core Ops, SparseCore 0:
  12.9 58.8 all-gather.10
  74.5 53.3 all-gather.6
  130.1 51.1 all-gather.12
  183.9 54.2 all-gather.8

commit v2 on v1

v2 whole, which is shorter than its diff:
```python
import functools

import jax
import jax.numpy as jnp
from jax import lax
from jax.experimental import pallas as pl
from jax.experimental.pallas import tpu as pltpu
from jax.sharding import PartitionSpec as P

D = 1152
HEADS = 16
HEAD_DIM = 72
MESH = pl.DeviceIdType.MESH
VMEM = pltpu.VMEM
LIMIT = 56 * 1024 * 1024


def add_gated(h, gate, branch):
    return (h.astype(jnp.float32) + gate * branch.astype(jnp.float32)).astype(jnp.bfloat16)


def modulate(h, shift, scale):
    x = h.astype(jnp.float32)
    mean = jnp.mean(x, axis=-1, keepdims=True)
    c = x - mean
    var = jnp.mean(c * c, axis=-1, keepdims=True)
    return (c * lax.rsqrt(var + 1e-06) * (1.0 + scale) + shift).astype(jnp.bfloat16)


def mod_row(mod_ref, step, attn, which):
    row = (step * 2 + attn) * 3 + which
    return mod_ref[row : row + 1, :]


def place():
    return lax.axis_index("tm"), lax.axis_index("space")


def device(t, s):
    return {"tm": t, "space": s}


def greet(peers):
    barrier = pltpu.get_barrier_semaphore()
    for t, s in peers:
        pl.semaphore_signal(barrier, inc=1, device_id=device(t, s), device_id_type=MESH)
    pl.semaphore_wait(barrier, len(peers))


def tm_peers(nt, t, s):
    return [(lax.rem(t + k, nt), s) for k in range(1, nt)]


def space_peers(ns, t, s):
    return [(t, lax.rem(s + k, ns)) for k in range(1, ns)]


def chip_peers(ns, s):
    return [lax.rem(s + 2 * k, ns) for k in range(1, ns // 2)], s + 1 - 2 * lax.rem(s, 2)


def remote(src, dst, send, recv, t, s):
    return pltpu.make_async_remote_copy(
        src_ref=src, dst_ref=dst, send_sem=send, recv_sem=recv, device_id=device(t, s), device_id_type=MESH
    )


class Spread:
    def __init__(self, slots, send, recv, ns, t, s, chunks):
        self.slots, self.send, self.recv, self.t, self.s, self.chunks = slots, send, recv, t, s, chunks
        self.others, self.sib = chip_peers(ns, s)
        self.started = []

    def copy(self, base, i, lane, n, to):
        ref = self.slots.at[base, i]
        return remote(ref, ref, self.send.at[lane, n], self.recv.at[base, i], self.t, to)

    def push(self, base, i, lane, n, to):
        c = self.copy(base, i, lane, n, to)
        c.start()
        self.started.append(c)

    def begin(self, ready=None):
        for n, i in enumerate(self.chunks):
            if ready is not None:
                ready(i)
            for k, o in enumerate(self.others):
                self.push(self.s, i, k, n, o)
            self.push(self.s, i, len(self.others), n, self.sib)

    def forward(self):
        for n, i in enumerate(self.chunks):
            for k, o in enumerate(self.others):
                self.copy(o, i, 0, 0, self.sib).wait_recv()
                self.push(o, i, len(self.others) + 1 + k, n, self.sib)

    def finish(self):
        for i in self.chunks:
            for base in [self.sib] + [o + self.sib - self.s for o in self.others]:
                self.copy(base, i, 0, 0, self.sib).wait_recv()

    def drain(self):
        for c in self.started:
            c.wait_send()


class Gather:
    def __init__(self, slots, send, recv, nt, t, s):
        self.slots, self.send, self.recv, self.s, self.t = slots, send, recv, s, t
        self.line = nt // 2
        self.z = t // 2
        self.pair = t + 1 - 2 * lax.rem(t, 2)
        self.stage_at = 0

    def copy(self, slot, kind, to):
        ref = self.slots.at[slot]
        return remote(ref, ref, self.send.at[kind, slot], self.recv.at[slot], to, self.s)

    def each(self, d, act, arrive):
        t, z, line = self.t, self.z, self.line

        def up(slot):
            pl.when(z + 1 < line)(lambda: act(self.copy(slot, 0, t + 2)))

        def down(slot):
            pl.when(z > 0)(lambda: act(self.copy(slot, 1, t - 2)))

        if d == 0:
            up(t)
            down(t)
            act(self.copy(t, 2, self.pair))
            return

        def from_below():
            slot = t - 2 * d
            if arrive:
                self.copy(slot, 2, self.pair).wait_recv()
            up(slot)
            act(self.copy(slot, 2, self.pair))

        def from_above():
            slot = t + 2 * d
            if arrive:
                self.copy(slot, 2, self.pair).wait_recv()
            down(slot)
            act(self.copy(slot, 2, self.pair))

        pl.when(z >= d)(from_below)
        pl.when(z + d < line)(from_above)

    def stage(self):
        if self.stage_at < self.line:
            self.each(self.stage_at, lambda c: c.start(), True)
            self.stage_at += 1

    def finish(self):
        while self.stage_at < self.line:
            self.stage()
        for z in range(self.line):
            self.copy(2 * z + 1 - lax.rem(self.t, 2), 2, self.pair).wait_recv()

    def drain(self):
        for d in range(self.line):
            self.each(d, lambda c: c.wait_send(), False)


def heads_of(qkv, heads):
    out = []
    for i in range(heads):
        parts = [qkv[:, (3 * i + j) * HEAD_DIM : (3 * i + j + 1) * HEAD_DIM] for j in range(3)]
        for j in range(2):
            sq = jnp.sum(parts[j] * parts[j], axis=-1, keepdims=True)
            parts[j] = parts[j] * lax.rsqrt(sq * (1.0 / HEAD_DIM) + 1e-06)
        out.append([p.astype(jnp.bfloat16) for p in parts])
    return out


def attend(q, k, v, mask):
    scores = lax.dot_general(q, k, (((1,), (1,)), ((), ())), preferred_element_type=jnp.float32)
    expo = jnp.exp(scores * (HEAD_DIM**-0.5))
    if mask is not None:
        expo = jnp.where(mask, expo, 0.0)
    probs = (expo / jnp.sum(expo, axis=-1, keepdims=True)).astype(jnp.bfloat16)
    return jnp.dot(probs, v, preferred_element_type=jnp.float32).astype(jnp.bfloat16)


def kernel(
    nt, ns, batch, lat, cache, mod, weights, block_out, new_s, new_t,
    x, x2, own, w, wo, mine, o, y, back, qs, ks, vs,
    send_w, recv_w, send_wo, recv_wo, send_a, send_x, recv_x, send_x2, recv_x2, send_o, recv_o, send_y, recv_y,
):
    t, s = place()
    heads = HEADS // ns
    rows = x.shape[1] * x.shape[2]
    block = rows // nt
    span = rows // batch
    out_cols, in_cols = D // ns, 3 * D // ns
    depth = weights.shape[1]

    for i in range(ns):

        @pl.when(s == i)
        def _():
            for a in range(2):
                w[a, t, :, :out_cols] = weights[a, :, 3 * D + i * out_cols : 3 * D + (i + 1) * out_cols]
                w[a, t, :, out_cols:] = weights[a, :, i * in_cols : (i + 1) * in_cols]

    greet(tm_peers(nt, t, s) + space_peers(ns, t, s))
    gathers = [Gather(w.at[a], send_w.at[a], recv_w.at[a], nt, t, s) for a in range(2)]
    first, second = gathers[1], gathers[0]
    first.stage()

    def spread_out(a):
        wo[a, s] = w[a, :, :, :out_cols].reshape(wo.shape[2:])
        return Spread(wo.at[a], send_wo.at[a], recv_wo.at[a], ns, t, s, list(range(wo.shape[2])))

    h = add_gated(lat[...], mod_row(mod, 0, 0, 2), cache[...])
    block_out[...] = h
    own[...] = modulate(h, mod_row(mod, 0, 1, 0), mod_row(mod, 0, 1, 1)).reshape(own.shape)
    started = []
    for k in range(1, nt):
        p = lax.rem(t + k, nt)
        c = remote(own.at[p], x.at[s, t], send_a.at[k], recv_x.at[s, t], p, s)
        c.start()
        started.append(c)
    x[s, t] = own[t]
    first.stage()

    def ready(q):
        if q is not t:
            remote(own.at[0], x.at[s, q], send_a.at[0], recv_x.at[s, q], t, s).wait_recv()

    tokens = Spread(x, send_x, recv_x, ns, t, s, [t] + [lax.rem(t + nt - k, nt) for k in range(1, nt)])
    tokens.begin(ready)
    first.stage()
    tokens.forward()
    first.finish()
    second.stage()
    out_t = spread_out(1)
    out_t.begin()
    tokens.finish()

    mask = lax.rem(lax.broadcasted_iota(jnp.int32, (rows, rows), 0), block) == lax.rem(
        lax.broadcasted_iota(jnp.int32, (rows, rows), 1), block
    )

    def projected(a, tokens_in):
        qkv = jnp.dot(tokens_in, w[a].reshape(nt * depth, out_cols + in_cols), preferred_element_type=jnp.float32)
        return heads_of(qkv[:, out_cols:], heads)

    def send_out(a, step, p):
        return remote(mine.at[a, p], o.at[a, s], send_o.at[a, step], recv_o.at[a, s], t, p)

    def temporal_tile(step, carry):
        p = lax.rem(s + step, ns)
        outs = [attend(q, k, v, mask) for q, k, v in projected(1, x[p].reshape(rows, D))]
        mine[1, p] = jnp.concatenate(outs, axis=-1)
        pl.when(step < ns)(lambda: send_out(1, step, p).start())
        return carry

    def collect(a):
        o[a, s] = mine[a, s]
        for k in range(1, ns):
            q = lax.rem(s + k, ns)
            remote(mine.at[a, q], o.at[a, q], send_o.at[a, k], recv_o.at[a, q], t, q).wait_recv()

    def project(a):
        attn = jnp.concatenate([o[a, i] for i in range(ns)], axis=-1)
        cols = [
            jnp.dot(attn, wo[a, i].reshape(D, out_cols), preferred_element_type=jnp.float32).astype(jnp.bfloat16)
            for i in range(ns)
        ]
        return jnp.concatenate(cols, axis=-1)

    lax.fori_loop(1, ns + 1, temporal_tile, 0)
    out_t.forward()
    second.stage()
    out_t.finish()
    collect(1)
    y[...] = project(1).reshape(y.shape)
    for k in range(1, nt):
        p = lax.rem(t + k, nt)
        c = remote(y.at[p], back.at[t], send_y.at[k], recv_y.at[t], p, s)
        c.start()
        started.append(c)
    back[t] = y[t]
    second.stage()
    for k in range(1, nt):
        q = lax.rem(t + k, nt)
        remote(y.at[q], back.at[q], send_y.at[k], recv_y.at[q], q, s).wait_recv()
    fresh = back[...].reshape(rows, D)
    new_t[...] = fresh
    h = add_gated(block_out[...], mod_row(mod, 0, 1, 2), fresh)
    block_out[...] = h
    x2[s] = modulate(h, mod_row(mod, 1, 0, 0), mod_row(mod, 1, 0, 1)).reshape(x2.shape[1:])
    tokens2 = Spread(x2, send_x2, recv_x2, ns, t, s, list(range(x2.shape[1])))
    tokens2.begin()
    second.finish()
    tokens2.forward()
    out_s = spread_out(0)
    out_s.begin()
    tokens2.finish()

    def proj(p, carry):
        for i, (q, k, v) in enumerate(projected(0, x2[p].reshape(rows, D))):
            for b in range(batch):
                part = slice(b * span, (b + 1) * span)
                qs[p, i, b] = q[part]
                ks[i, b, p] = k[part]
                vs[i, b, p] = v[part]
        return carry

    lax.fori_loop(0, ns, proj, 0)

    def spatial_tile(step, carry):
        p = lax.rem(s + step, ns)
        for b in range(batch):
            outs = []
            for i in range(heads):
                keys = ks[i, b].reshape(ns * span, HEAD_DIM)
                vals = vs[i, b].reshape(ns * span, HEAD_DIM)
                outs.append(attend(qs[p, i, b], keys, vals, None))
            mine[0, p, b * span : (b + 1) * span, :] = jnp.concatenate(outs, axis=-1)
        pl.when(step < ns)(lambda: send_out(0, step, p).start())
        return carry

    lax.fori_loop(1, ns + 1, spatial_tile, 0)
    out_s.forward()
    out_s.finish()
    collect(0)
    fresh = project(0)
    new_s[...] = fresh
    h = add_gated(block_out[...], mod_row(mod, 1, 0, 2), fresh)
    block_out[...] = add_gated(h, mod_row(mod, 1, 1, 2), new_t[...])
    for a in range(2):
        for k in range(1, ns):
            send_out(a, k, lax.rem(s + k, ns)).wait_send()
    for c in started:
        c.wait_send()
    for part in [first, second, out_t, out_s, tokens, tokens2]:
        part.drain()


def shards(nt, ns, latent, spatial_cache, modulation, weights):
    batch, _, span, _ = latent.shape
    rows = batch * span
    block = rows // nt
    depth = weights.shape[1]
    heads = HEADS // ns
    dma = pltpu.SemaphoreType.DMA
    chunks, out_chunks = 8, 2

    def vmem(*shape):
        return VMEM(shape, jnp.bfloat16)

    args = (latent.reshape(rows, D), spatial_cache.reshape(rows, D), modulation.reshape(12, D), weights)
    outs = pl.pallas_call(
        functools.partial(kernel, nt, ns, batch),
        out_shape=[jax.ShapeDtypeStruct((rows, D), jnp.bfloat16)] * 3,
        in_specs=[pl.BlockSpec(memory_space=VMEM)] * len(args),
        out_specs=[pl.BlockSpec(memory_space=VMEM)] * 3,
        scratch_shapes=[
            vmem(ns, nt, block, D),
            vmem(ns, chunks, rows // chunks, D),
            vmem(nt, block, D),
            vmem(2, nt, depth, 4 * D // ns),
            vmem(2, ns, out_chunks, D // out_chunks, D // ns),
            vmem(2, ns, rows, D // ns),
            vmem(2, ns, rows, D // ns),
            vmem(nt, block, D),
            vmem(nt, block, D),
            vmem(ns, heads, batch, span, HEAD_DIM),
            vmem(heads, batch, ns, span, HEAD_DIM),
            vmem(heads, batch, ns, span, HEAD_DIM),
            dma((2, 3, nt)),
            dma((2, nt)),
            dma((2, ns, out_chunks)),
            dma((2, ns, out_chunks)),
            dma((nt,)),
            dma((ns, nt)),
            dma((ns, nt)),
            dma((ns, chunks)),
            dma((ns, chunks)),
            dma((2, ns)),
            dma((2, ns)),
            dma((nt,)),
            dma((nt,)),
        ],
        cost_estimate=pl.CostEstimate(flops=6_000_000_000, bytes_accessed=20_000_000, transcendentals=4_000_000),
        compiler_params=pltpu.CompilerParams(
            collective_id=0, has_side_effects=True, vmem_limit_bytes=LIMIT
        ),
    )(*args)
    return tuple(a.reshape(latent.shape) for a in outs)


def solution(mesh):
    part = P(None, "tm", "space", None)
    return jax.shard_map(
        functools.partial(shards, mesh.shape["tm"], mesh.shape["space"]),
        mesh=mesh,
        in_specs=(part, part, P(), P(None, "tm", None)),
        out_specs=(part, part, part),
        check_vma=False,
    )
```

time: 280 us -> 145 us (0.52)
  the two profiles are of different devices: /device:TPU:1 before, /device:TPU:31 now
where the time goes in v2:
time: 145 us
  Pallas kernels  138 us (95%)
  local copies, waits for them, and re-layouts  6.23 us (4%)
    pallas_call x1, Pallas kernels, shards(): pl.pallas_call(functools.partial(kernel, nt, ns, batch), out_shape=[jax.S...  138 us
    unnamed x6, local copies, waits for them, and re-layouts  5.57 us

profile of v2, /device:TPU:31, one launch (start us, length us, event | category | flops | bytes accessed | tf_op | source)
XLA Modules:
  0.0 144.9 jit_solution(15376985489002329902)
XLA Ops:
  0.6 0.8 copy.11
  1.5 0.7 reshape.26.mod
  2.1 138.0 %shard_map.67 = (bf16[256,1152]{1,0:T(8,128)(2,1)}, bf16[256,1152]{1,0:T(8,128)(2,1)}, bf16[256,1152]{1,0:T(8,128)(2,1)}) custom-call(bf16[256,1152]{1,0:T(8,128)(2,1)} %bitcast.14, bf16[256,1152]{1,0:T(8,128)(2,1)} %bitcast.15, f32[12,1152]{1,0:T(8,128)} %reshape.26.mod, bf16[2,144,4608]{2,1,0:T(8,128)(2,1)} %weights.1), custom_call_target="tpu_custom_call" | custom-call | flops 6000000000 | bytes 20000000 | tf_op jit(solution)/shard_map/pallas_call | solution.py:357
  140.1 0.0 copy-start
  140.1 2.0 %copy.18 = bf16[2,1,128,1152]{3,2,1,0:T(8,128)(2,1)} copy(bf16[2,1,128,1152]{3,2,1,0:T(8,128)(2,1)} %bitcast.13) | data formatting | bytes 1179648
  142.1 1.9 %copy.19 = bf16[2,1,128,1152]{3,2,1,0:T(8,128)(2,1)} copy(bf16[2,1,128,1152]{3,2,1,0:T(8,128)(2,1)} %bitcast.12) | data formatting | bytes 1179648
  144.1 0.0 copy-done
  144.1 0.8 copy.20
Async XLA Ops:
  140.1 3.9 %copy-start = (bf16[256,1152]{1,0:T(8,128)(2,1)S(1)}, bf16[256,1152]{1,0:T(8,128)(2,1)}, u32[]{:S(2)}) copy-start(bf16[256,1152]{1,0:T(8,128)(2,1)} %get-tuple-element.8) | copy-start | bytes 1769476

commit v3 on v2

--- a/solution.py
+++ b/solution.py
@@ -80,8 +80,8 @@
         c.start()
         self.started.append(c)
 
-    def begin(self, ready=None):
-        for n, i in enumerate(self.chunks):
+    def begin(self, ready=None, first=0, last=None):
+        for n, i in list(enumerate(self.chunks))[first:last]:
             if ready is not None:
                 ready(i)
             for k, o in enumerate(self.others):
@@ -186,8 +186,8 @@
 
 def kernel(
     nt, ns, batch, lat, cache, mod, weights, block_out, new_s, new_t,
-    x, x2, own, w, wo, mine, o, y, back, qs, ks, vs,
-    send_w, recv_w, send_wo, recv_wo, send_a, send_x, recv_x, send_x2, recv_x2, send_o, recv_o, send_y, recv_y,
+    x, x2, own, w, v, wo, mine, o, y, back, qs, ks, vs,
+    send_w, recv_w, send_v, recv_v, send_wo, recv_wo, send_a, send_x, recv_x, send_x2, recv_x2, send_o, recv_o, send_y, recv_y,
 ):
     t, s = place()
     heads = HEADS // ns
@@ -202,16 +202,19 @@
         @pl.when(s == i)
         def _():
             for a in range(2):
-                w[a, t, :, :out_cols] = weights[a, :, 3 * D + i * out_cols : 3 * D + (i + 1) * out_cols]
-                w[a, t, :, out_cols:] = weights[a, :, i * in_cols : (i + 1) * in_cols]
+                v[a, t] = weights[a, :, 3 * D + i * out_cols : 3 * D + (i + 1) * out_cols]
+                w[a, t] = weights[a, :, i * in_cols : (i + 1) * in_cols]
 
     greet(tm_peers(nt, t, s) + space_peers(ns, t, s))
-    gathers = [Gather(w.at[a], send_w.at[a], recv_w.at[a], nt, t, s) for a in range(2)]
-    first, second = gathers[1], gathers[0]
-    first.stage()
+    qkv_s, qkv_t = [Gather(w.at[a], send_w.at[a], recv_w.at[a], nt, t, s) for a in range(2)]
+    cols_s, cols_t = [Gather(v.at[a], send_v.at[a], recv_v.at[a], nt, t, s) for a in range(2)]
+    qkv_t.stage()
+
+    def fold(part, axis_in, axis_out):
+        return jnp.concatenate(jnp.split(part, ns, axis=axis_in), axis=axis_out)
 
     def spread_out(a):
-        wo[a, s] = w[a, :, :, :out_cols].reshape(wo.shape[2:])
+        wo[a, s] = fold(v[a].reshape(D, out_cols), 0, 1).reshape(wo.shape[2:])
         return Spread(wo.at[a], send_wo.at[a], recv_wo.at[a], ns, t, s, list(range(wo.shape[2])))
 
     h = add_gated(lat[...], mod_row(mod, 0, 0, 2), cache[...])
@@ -224,20 +227,20 @@
         c.start()
         started.append(c)
     x[s, t] = own[t]
-    first.stage()
+    qkv_t.stage()
 
     def ready(q):
         if q is not t:
             remote(own.at[0], x.at[s, q], send_a.at[0], recv_x.at[s, q], t, s).wait_recv()
 
     tokens = Spread(x, send_x, recv_x, ns, t, s, [t] + [lax.rem(t + nt - k, nt) for k in range(1, nt)])
-    tokens.begin(ready)
-    first.stage()
+    tokens.begin(ready, 0, nt // 2)
+    qkv_t.stage()
+    tokens.begin(ready, nt // 2, nt)
+    qkv_t.stage()
+    cols_t.stage()
     tokens.forward()
-    first.finish()
-    second.stage()
-    out_t = spread_out(1)
-    out_t.begin()
+    qkv_t.finish()
     tokens.finish()
 
     mask = lax.rem(lax.broadcasted_iota(jnp.int32, (rows, rows), 0), block) == lax.rem(
@@ -245,8 +248,8 @@
     )
 
     def projected(a, tokens_in):
-        qkv = jnp.dot(tokens_in, w[a].reshape(nt * depth, out_cols + in_cols), preferred_element_type=jnp.float32)
-        return heads_of(qkv[:, out_cols:], heads)
+        qkv = jnp.dot(tokens_in, w[a].reshape(nt * depth, in_cols), preferred_element_type=jnp.float32)
+        return heads_of(qkv, heads)
 
     def send_out(a, step, p):
         return remote(mine.at[a, p], o.at[a, s], send_o.at[a, step], recv_o.at[a, s], t, p)
@@ -254,8 +257,11 @@
     def temporal_tile(step, carry):
         p = lax.rem(s + step, ns)
         outs = [attend(q, k, v, mask) for q, k, v in projected(1, x[p].reshape(rows, D))]
-        mine[1, p] = jnp.concatenate(outs, axis=-1)
+        mine[1, p] = fold(jnp.concatenate(outs, axis=-1), 0, 1)
         pl.when(step < ns)(lambda: send_out(1, step, p).start())
+        pl.when(step == 1)(cols_t.stage)
+        pl.when(step == 2)(cols_t.stage)
+        pl.when(step == 3)(lambda: (cols_t.stage(), cols_s.stage()) and None)
         return carry
 
     def collect(a):
@@ -265,18 +271,25 @@
             remote(mine.at[a, q], o.at[a, q], send_o.at[a, k], recv_o.at[a, q], t, q).wait_recv()
 
     def project(a):
-        attn = jnp.concatenate([o[a, i] for i in range(ns)], axis=-1)
-        cols = [
-            jnp.dot(attn, wo[a, i].reshape(D, out_cols), preferred_element_type=jnp.float32).astype(jnp.bfloat16)
-            for i in range(ns)
-        ]
+        attn = jnp.concatenate([fold(o[a, i], 1, 0) for i in range(ns)], axis=-1)
+        cols = []
+        for i in range(ns):
+            weight = fold(wo[a, i].reshape(out_cols, D), 1, 0)
+            cols.append(jnp.dot(attn, weight, preferred_element_type=jnp.float32).astype(jnp.bfloat16))
         return jnp.concatenate(cols, axis=-1)
 
     lax.fori_loop(1, ns + 1, temporal_tile, 0)
+    cols_t.finish()
+    out_t = spread_out(1)
+    out_t.begin()
+    cols_s.stage()
+    qkv_s.stage()
+    collect(1)
+    cols_s.stage()
     out_t.forward()
-    second.stage()
+    cols_s.stage()
+    qkv_s.stage()
     out_t.finish()
-    collect(1)
     y[...] = project(1).reshape(y.shape)
     for k in range(1, nt):
         p = lax.rem(t + k, nt)
@@ -284,7 +297,10 @@
         c.start()
         started.append(c)
     back[t] = y[t]
-    second.stage()
+    cols_s.finish()
+    out_s = spread_out(0)
+    out_s.begin()
+    qkv_s.stage()
     for k in range(1, nt):
         q = lax.rem(t + k, nt)
         remote(y.at[q], back.at[q], send_y.at[k], recv_y.at[q], q, s).wait_recv()
@@ -295,13 +311,13 @@
     x2[s] = modulate(h, mod_row(mod, 1, 0, 0), mod_row(mod, 1, 0, 1)).reshape(x2.shape[1:])
     tokens2 = Spread(x2, send_x2, recv_x2, ns, t, s, list(range(x2.shape[1])))
     tokens2.begin()
-    second.finish()
+    qkv_s.stage()
+    out_s.forward()
     tokens2.forward()
-    out_s = spread_out(0)
-    out_s.begin()
-    tokens2.finish()
+    qkv_s.finish()
 
     def proj(p, carry):
+        p = lax.rem(s + p, ns)
         for i, (q, k, v) in enumerate(projected(0, x2[p].reshape(rows, D))):
             for b in range(batch):
                 part = slice(b * span, (b + 1) * span)
@@ -310,22 +326,25 @@
                 vs[i, b, p] = v[part]
         return carry
 
-    lax.fori_loop(0, ns, proj, 0)
+    proj(0, 0)
+    tokens2.finish()
+    lax.fori_loop(1, ns, proj, 0)
 
     def spatial_tile(step, carry):
         p = lax.rem(s + step, ns)
+        parts = []
         for b in range(batch):
             outs = []
             for i in range(heads):
                 keys = ks[i, b].reshape(ns * span, HEAD_DIM)
                 vals = vs[i, b].reshape(ns * span, HEAD_DIM)
                 outs.append(attend(qs[p, i, b], keys, vals, None))
-            mine[0, p, b * span : (b + 1) * span, :] = jnp.concatenate(outs, axis=-1)
+            parts.append(jnp.concatenate(outs, axis=-1))
+        mine[0, p] = fold(jnp.concatenate(parts, axis=0), 0, 1)
         pl.when(step < ns)(lambda: send_out(0, step, p).start())
         return carry
 
     lax.fori_loop(1, ns + 1, spatial_tile, 0)
-    out_s.forward()
     out_s.finish()
     collect(0)
     fresh = project(0)
@@ -337,7 +356,7 @@
             send_out(a, k, lax.rem(s + k, ns)).wait_send()
     for c in started:
         c.wait_send()
-    for part in [first, second, out_t, out_s, tokens, tokens2]:
+    for part in [qkv_t, cols_t, qkv_s, cols_s, out_t, out_s, tokens, tokens2]:
         part.drain()
 
 
@@ -348,7 +367,7 @@
     depth = weights.shape[1]
     heads = HEADS // ns
     dma = pltpu.SemaphoreType.DMA
-    chunks, out_chunks = 8, 2
+    chunks, out_chunks = 8, 2 if D // ns % 32 == 0 else 1
 
     def vmem(*shape):
         return VMEM(shape, jnp.bfloat16)
@@ -363,15 +382,18 @@
             vmem(ns, nt, block, D),
             vmem(ns, chunks, rows // chunks, D),
             vmem(nt, block, D),
-            vmem(2, nt, depth, 4 * D // ns),
-            vmem(2, ns, out_chunks, D // out_chunks, D // ns),
-            vmem(2, ns, rows, D // ns),
-            vmem(2, ns, rows, D // ns),
+            vmem(2, nt, depth, 3 * D // ns),
+            vmem(2, nt, depth, D // ns),
+            vmem(2, ns, out_chunks, D // ns // out_chunks, D),
+            vmem(2, ns, rows // ns, D),
+            vmem(2, ns, rows // ns, D),
             vmem(nt, block, D),
             vmem(nt, block, D),
             vmem(ns, heads, batch, span, HEAD_DIM),
             vmem(heads, batch, ns, span, HEAD_DIM),
             vmem(heads, batch, ns, span, HEAD_DIM),
+            dma((2, 3, nt)),
+            dma((2, nt)),
             dma((2, 3, nt)),
             dma((2, nt)),
             dma((2, ns, out_chunks)),

time: 145 us -> 142 us (0.979)
  the two profiles are of different devices: /device:TPU:31 before, /device:TPU:1 now
where the time goes in v3:
time: 142 us; the launch traced here: 141 us
  Pallas kernels  134 us (94%)
  local copies, waits for them, and re-layouts  6.23 us (4%)
    pallas_call x1, Pallas kernels, shards(): pl.pallas_call(functools.partial(kernel, nt, ns, batch), out_shape=[jax.S...  134 us
    unnamed x6, local copies, waits for them, and re-layouts  5.57 us

profile of v3, /device:TPU:1, one launch (start us, length us, event | category | flops | bytes accessed | tf_op | source)
XLA Modules:
  0.0 141.3 jit_solution(2923874131782517165)
XLA Ops:
  0.6 0.8 copy.11
  1.5 0.7 reshape.26.mod
  2.1 134.4 %shard_map.67 = (bf16[256,1152]{1,0:T(8,128)(2,1)}, bf16[256,1152]{1,0:T(8,128)(2,1)}, bf16[256,1152]{1,0:T(8,128)(2,1)}) custom-call(bf16[256,1152]{1,0:T(8,128)(2,1)} %bitcast.14, bf16[256,1152]{1,0:T(8,128)(2,1)} %bitcast.15, f32[12,1152]{1,0:T(8,128)} %reshape.26.mod, bf16[2,144,4608]{2,1,0:T(8,128)(2,1)} %weights.1), custom_call_target="tpu_custom_call" | custom-call | flops 6000000000 | bytes 20000000 | tf_op jit(solution)/shard_map/pallas_call | solution.py:376
  136.6 0.0 copy-start
  136.6 2.0 %copy.18 = bf16[2,1,128,1152]{3,2,1,0:T(8,128)(2,1)} copy(bf16[2,1,128,1152]{3,2,1,0:T(8,128)(2,1)} %bitcast.13) | data formatting | bytes 1179648
  138.5 1.9 %copy.19 = bf16[2,1,128,1152]{3,2,1,0:T(8,128)(2,1)} copy(bf16[2,1,128,1152]{3,2,1,0:T(8,128)(2,1)} %bitcast.12) | data formatting | bytes 1179648
  140.5 0.0 copy-done
  140.5 0.8 copy.20
Async XLA Ops:
  136.6 3.9 %copy-start = (bf16[256,1152]{1,0:T(8,128)(2,1)S(1)}, bf16[256,1152]{1,0:T(8,128)(2,1)}, u32[]{:S(2)}) copy-start(bf16[256,1152]{1,0:T(8,128)(2,1)} %get-tuple-element.8) | copy-start | bytes 1769476

commit v4 on v3

--- a/solution.py
+++ b/solution.py
@@ -10,6 +10,9 @@
 D = 1152
 HEADS = 16
 HEAD_DIM = 72
+LANES = 128
+LOG2E = 1.4426950408889634
+QUERIES = 512
 MESH = pl.DeviceIdType.MESH
 VMEM = pltpu.VMEM
 LIMIT = 56 * 1024 * 1024
@@ -177,17 +180,21 @@
 
 def attend(q, k, v, mask):
     scores = lax.dot_general(q, k, (((1,), (1,)), ((), ())), preferred_element_type=jnp.float32)
-    expo = jnp.exp(scores * (HEAD_DIM**-0.5))
+    expo = jnp.exp2(scores * (HEAD_DIM**-0.5 * LOG2E)).astype(jnp.bfloat16)
     if mask is not None:
-        expo = jnp.where(mask, expo, 0.0)
-    probs = (expo / jnp.sum(expo, axis=-1, keepdims=True)).astype(jnp.bfloat16)
-    return jnp.dot(probs, v, preferred_element_type=jnp.float32).astype(jnp.bfloat16)
+        expo = expo * mask
+    out = jnp.dot(expo, v, preferred_element_type=jnp.float32)
+    return (out[:, :HEAD_DIM] * (1.0 / out[:, HEAD_DIM : HEAD_DIM + 1])).astype(jnp.bfloat16)
+
+
+def with_ones(v):
+    return jnp.concatenate([v, jnp.ones((v.shape[0], LANES - HEAD_DIM), v.dtype)], axis=-1)
 
 
 def kernel(
     nt, ns, batch, lat, cache, mod, weights, block_out, new_s, new_t,
-    x, x2, own, w, v, wo, mine, o, y, back, qs, ks, vs,
-    send_w, recv_w, send_v, recv_v, send_wo, recv_wo, send_a, send_x, recv_x, send_x2, recv_x2, send_o, recv_o, send_y, recv_y,
+    x, x2, own, w, v, wo, mine, o, mine_s, o_s, y, back, qs, ks, vs,
+    send_w, recv_w, send_v, recv_v, send_wo, recv_wo, send_a, send_x, recv_x, send_x2, recv_x2, send_o, recv_o, send_s, recv_s, send_y, recv_y,
 ):
     t, s = place()
     heads = HEADS // ns
@@ -246,32 +253,45 @@
     mask = lax.rem(lax.broadcasted_iota(jnp.int32, (rows, rows), 0), block) == lax.rem(
         lax.broadcasted_iota(jnp.int32, (rows, rows), 1), block
     )
+    mask = jnp.where(mask, 1.0, 0.0).astype(jnp.bfloat16)
 
     def projected(a, tokens_in):
         qkv = jnp.dot(tokens_in, w[a].reshape(nt * depth, in_cols), preferred_element_type=jnp.float32)
         return heads_of(qkv, heads)
 
-    def send_out(a, step, p):
-        return remote(mine.at[a, p], o.at[a, s], send_o.at[a, step], recv_o.at[a, s], t, p)
+    def send_out(step, p):
+        return remote(mine.at[p], o.at[s], send_o.at[step], recv_o.at[s], t, p)
+
+    def send_batch(b, k):
+        q = lax.rem(s + k, ns)
+        return remote(mine_s.at[b, q], o_s.at[b, s], send_s.at[b, k], recv_s.at[b, s], t, q)
+
+    groups = span // mine_s.shape[2]
+
+    def fold_rows(part):
+        return jnp.concatenate(jnp.split(part, groups, axis=0), axis=1)
+
+    def unfold_rows(part):
+        return jnp.concatenate(jnp.split(part, groups, axis=1), axis=0)
 
     def temporal_tile(step, carry):
         p = lax.rem(s + step, ns)
-        outs = [attend(q, k, v, mask) for q, k, v in projected(1, x[p].reshape(rows, D))]
-        mine[1, p] = fold(jnp.concatenate(outs, axis=-1), 0, 1)
-        pl.when(step < ns)(lambda: send_out(1, step, p).start())
+        outs = [attend(q, k, with_ones(v), mask) for q, k, v in projected(1, x[p].reshape(rows, D))]
+        mine[p] = fold(jnp.concatenate(outs, axis=-1), 0, 1)
+        pl.when(step < ns)(lambda: send_out(step, p).start())
         pl.when(step == 1)(cols_t.stage)
         pl.when(step == 2)(cols_t.stage)
         pl.when(step == 3)(lambda: (cols_t.stage(), cols_s.stage()) and None)
         return carry
 
-    def collect(a):
-        o[a, s] = mine[a, s]
+    def collect():
+        o[s] = mine[s]
         for k in range(1, ns):
             q = lax.rem(s + k, ns)
-            remote(mine.at[a, q], o.at[a, q], send_o.at[a, k], recv_o.at[a, q], t, q).wait_recv()
-
-    def project(a):
-        attn = jnp.concatenate([fold(o[a, i], 1, 0) for i in range(ns)], axis=-1)
+            remote(mine.at[q], o.at[q], send_o.at[k], recv_o.at[q], t, q).wait_recv()
+
+    def project(a, parts):
+        attn = jnp.concatenate(parts, axis=-1)
         cols = []
         for i in range(ns):
             weight = fold(wo[a, i].reshape(out_cols, D), 1, 0)
@@ -284,13 +304,13 @@
     out_t.begin()
     cols_s.stage()
     qkv_s.stage()
-    collect(1)
+    collect()
     cols_s.stage()
     out_t.forward()
     cols_s.stage()
     qkv_s.stage()
     out_t.finish()
-    y[...] = project(1).reshape(y.shape)
+    y[...] = project(1, [fold(o[i], 1, 0) for i in range(ns)]).reshape(y.shape)
     for k in range(1, nt):
         p = lax.rem(t + k, nt)
         c = remote(y.at[p], back.at[t], send_y.at[k], recv_y.at[t], p, s)
@@ -301,16 +321,18 @@
     out_s = spread_out(0)
     out_s.begin()
     qkv_s.stage()
-    for k in range(1, nt):
-        q = lax.rem(t + k, nt)
-        remote(y.at[q], back.at[q], send_y.at[k], recv_y.at[q], q, s).wait_recv()
-    fresh = back[...].reshape(rows, D)
-    new_t[...] = fresh
-    h = add_gated(block_out[...], mod_row(mod, 0, 1, 2), fresh)
-    block_out[...] = h
-    x2[s] = modulate(h, mod_row(mod, 1, 0, 0), mod_row(mod, 1, 0, 1)).reshape(x2.shape[1:])
-    tokens2 = Spread(x2, send_x2, recv_x2, ns, t, s, list(range(x2.shape[1])))
-    tokens2.begin()
+
+    def returned(q):
+        if q is not t:
+            remote(y.at[q], back.at[q], send_y.at[0], recv_y.at[q], t, s).wait_recv()
+        at = pl.ds(pl.multiple_of(q * block, block), block)
+        new_t[at, :] = back[q]
+        h = add_gated(block_out[at, :], mod_row(mod, 0, 1, 2), back[q])
+        block_out[at, :] = h
+        x2[s, q] = modulate(h, mod_row(mod, 1, 0, 0), mod_row(mod, 1, 0, 1))
+
+    tokens2 = Spread(x2, send_x2, recv_x2, ns, t, s, [t] + [lax.rem(t + nt - k, nt) for k in range(1, nt)])
+    tokens2.begin(returned)
     qkv_s.stage()
     out_s.forward()
     tokens2.forward()
@@ -321,39 +343,47 @@
         for i, (q, k, v) in enumerate(projected(0, x2[p].reshape(rows, D))):
             for b in range(batch):
                 part = slice(b * span, (b + 1) * span)
-                qs[p, i, b] = q[part]
+                qs[i, b, p] = q[part]
                 ks[i, b, p] = k[part]
-                vs[i, b, p] = v[part]
+                vs[i, b, p] = with_ones(v[part])
         return carry
 
     proj(0, 0)
     tokens2.finish()
     lax.fori_loop(1, ns, proj, 0)
 
-    def spatial_tile(step, carry):
-        p = lax.rem(s + step, ns)
-        parts = []
-        for b in range(batch):
-            outs = []
-            for i in range(heads):
-                keys = ks[i, b].reshape(ns * span, HEAD_DIM)
-                vals = vs[i, b].reshape(ns * span, HEAD_DIM)
-                outs.append(attend(qs[p, i, b], keys, vals, None))
-            parts.append(jnp.concatenate(outs, axis=-1))
-        mine[0, p] = fold(jnp.concatenate(parts, axis=0), 0, 1)
-        pl.when(step < ns)(lambda: send_out(0, step, p).start())
+    def spatial_batch(b, carry):
+        total = ns * span
+        step = min(QUERIES, total)
+        parts = [[] for _ in range(total // step)]
+        for i in range(heads):
+            queries = qs[i, b].reshape(total, HEAD_DIM)
+            keys = ks[i, b].reshape(total, HEAD_DIM)
+            vals = vs[i, b].reshape(total, LANES)
+            for j, part in enumerate(parts):
+                part.append(attend(queries[j * step : (j + 1) * step], keys, vals, None))
+        attn = jnp.concatenate([jnp.concatenate(part, axis=-1) for part in parts], axis=0)
+        for i in range(ns):
+            mine_s[b, i] = fold_rows(attn[i * span : (i + 1) * span])
+        for k in range(1, ns):
+            send_batch(b, k).start()
         return carry
 
-    lax.fori_loop(1, ns + 1, spatial_tile, 0)
+    lax.fori_loop(0, batch, spatial_batch, 0)
+    for b in range(batch):
+        o_s[b, s] = mine_s[b, s]
+        for k in range(1, ns):
+            q = lax.rem(s + k, ns)
+            remote(mine_s.at[b, q], o_s.at[b, q], send_s.at[b, k], recv_s.at[b, q], t, q).wait_recv()
     out_s.finish()
-    collect(0)
-    fresh = project(0)
+    fresh = project(0, [jnp.concatenate([unfold_rows(o_s[b, i]) for b in range(batch)], axis=0) for i in range(ns)])
     new_s[...] = fresh
     h = add_gated(block_out[...], mod_row(mod, 1, 0, 2), fresh)
     block_out[...] = add_gated(h, mod_row(mod, 1, 1, 2), new_t[...])
-    for a in range(2):
-        for k in range(1, ns):
-            send_out(a, k, lax.rem(s + k, ns)).wait_send()
+    for k in range(1, ns):
+        send_out(k, lax.rem(s + k, ns)).wait_send()
+        for b in range(batch):
+            send_batch(b, k).wait_send()
     for c in started:
         c.wait_send()
     for part in [qkv_t, cols_t, qkv_s, cols_s, out_t, out_s, tokens, tokens2]:
@@ -367,7 +397,8 @@
     depth = weights.shape[1]
     heads = HEADS // ns
     dma = pltpu.SemaphoreType.DMA
-    chunks, out_chunks = 8, 2 if D // ns % 32 == 0 else 1
+    out_chunks = 2 if D // ns % 32 == 0 else 1
+    groups = min(ns, span // 16)
 
     def vmem(*shape):
         return VMEM(shape, jnp.bfloat16)
@@ -380,18 +411,20 @@
         out_specs=[pl.BlockSpec(memory_space=VMEM)] * 3,
         scratch_shapes=[
             vmem(ns, nt, block, D),
-            vmem(ns, chunks, rows // chunks, D),
+            vmem(ns, nt, block, D),
             vmem(nt, block, D),
             vmem(2, nt, depth, 3 * D // ns),
             vmem(2, nt, depth, D // ns),
             vmem(2, ns, out_chunks, D // ns // out_chunks, D),
-            vmem(2, ns, rows // ns, D),
-            vmem(2, ns, rows // ns, D),
+            vmem(ns, rows // ns, D),
+            vmem(ns, rows // ns, D),
+            vmem(batch, ns, span // groups, D // ns * groups),
+            vmem(batch, ns, span // groups, D // ns * groups),
             vmem(nt, block, D),
             vmem(nt, block, D),
-            vmem(ns, heads, batch, span, HEAD_DIM),
             vmem(heads, batch, ns, span, HEAD_DIM),
             vmem(heads, batch, ns, span, HEAD_DIM),
+            vmem(heads, batch, ns, span, LANES),
             dma((2, 3, nt)),
             dma((2, nt)),
             dma((2, 3, nt)),
@@ -401,10 +434,12 @@
             dma((nt,)),
             dma((ns, nt)),
             dma((ns, nt)),
-            dma((ns, chunks)),
-            dma((ns, chunks)),
-            dma((2, ns)),
-            dma((2, ns)),
+            dma((ns, nt)),
+            dma((ns, nt)),
+            dma((ns,)),
+            dma((ns,)),
+            dma((batch, ns)),
+            dma((batch, ns)),
             dma((nt,)),
             dma((nt,)),
         ],

time: 142 us -> 137 us (0.965)
  Pallas kernels: 134 us -> 130 us
    pallas_call x1, Pallas kernels: 134 us -> 130 us  [shards(): pl.pallas_call(functools.partial(kernel, nt, ns, batch), out_shape=[jax.S...]
where the time goes in v4:
time: 137 us; the launch traced here: 136 us
  Pallas kernels  130 us (95%)
  local copies, waits for them, and re-layouts  6.23 us (5%)
    pallas_call x1, Pallas kernels, shards(): pl.pallas_call(functools.partial(kernel, nt, ns, batch), out_shape=[jax.S...  130 us
    unnamed x6, local copies, waits for them, and re-layouts  5.57 us

profile of v4, /device:TPU:1, one launch (start us, length us, event | category | flops | bytes accessed | tf_op | source)
XLA Modules:
  0.0 136.4 jit_solution(17424612575003381924)
XLA Ops:
  0.6 0.8 copy.11
  1.5 0.7 reshape.26.mod
  2.1 129.5 %shard_map.67 = (bf16[256,1152]{1,0:T(8,128)(2,1)}, bf16[256,1152]{1,0:T(8,128)(2,1)}, bf16[256,1152]{1,0:T(8,128)(2,1)}) custom-call(bf16[256,1152]{1,0:T(8,128)(2,1)} %bitcast.14, bf16[256,1152]{1,0:T(8,128)(2,1)} %bitcast.15, f32[12,1152]{1,0:T(8,128)} %reshape.26.mod, bf16[2,144,4608]{2,1,0:T(8,128)(2,1)} %weights.1), custom_call_target="tpu_custom_call" | custom-call | flops 6000000000 | bytes 20000000 | tf_op jit(solution)/shard_map/pallas_call | solution.py:407
  131.7 0.0 copy-start
  131.7 2.0 %copy.18 = bf16[2,1,128,1152]{3,2,1,0:T(8,128)(2,1)} copy(bf16[2,1,128,1152]{3,2,1,0:T(8,128)(2,1)} %bitcast.13) | data formatting | bytes 1179648
  133.7 1.9 %copy.19 = bf16[2,1,128,1152]{3,2,1,0:T(8,128)(2,1)} copy(bf16[2,1,128,1152]{3,2,1,0:T(8,128)(2,1)} %bitcast.12) | data formatting | bytes 1179648
  135.6 0.0 copy-done
  135.6 0.8 copy.20
Async XLA Ops:
  131.7 3.9 %copy-start = (bf16[256,1152]{1,0:T(8,128)(2,1)S(1)}, bf16[256,1152]{1,0:T(8,128)(2,1)}, u32[]{:S(2)}) copy-start(bf16[256,1152]{1,0:T(8,128)(2,1)} %get-tuple-element.8) | copy-start | bytes 1769476

commit v5 on v4

--- a/solution.py
+++ b/solution.py
@@ -31,8 +31,7 @@
 
 
 def mod_row(mod_ref, step, attn, which):
-    row = (step * 2 + attn) * 3 + which
-    return mod_ref[row : row + 1, :]
+    return mod_ref[step, attn, which : which + 1, :]
 
 
 def place():
@@ -390,6 +389,11 @@
         part.drain()
 
 
+def leave_kernel(*refs):
+    for i in range(3):
+        refs[3 + i][...] = refs[i][...]
+
+
 def shards(nt, ns, latent, spatial_cache, modulation, weights):
     batch, _, span, _ = latent.shape
     rows = batch * span
@@ -403,7 +407,7 @@
     def vmem(*shape):
         return VMEM(shape, jnp.bfloat16)
 
-    args = (latent.reshape(rows, D), spatial_cache.reshape(rows, D), modulation.reshape(12, D), weights)
+    args = (latent.reshape(rows, D), spatial_cache.reshape(rows, D), modulation, weights)
     outs = pl.pallas_call(
         functools.partial(kernel, nt, ns, batch),
         out_shape=[jax.ShapeDtypeStruct((rows, D), jnp.bfloat16)] * 3,
@@ -448,6 +452,13 @@
             collective_id=0, has_side_effects=True, vmem_limit_bytes=LIMIT
         ),
     )(*args)
+    outs = pl.pallas_call(
+        leave_kernel,
+        grid=(2,),
+        out_shape=[jax.ShapeDtypeStruct((rows, D), jnp.bfloat16)] * 3,
+        in_specs=[pl.BlockSpec((rows // 2, D), lambda i: (i, 0))] * 3,
+        out_specs=[pl.BlockSpec((rows // 2, D), lambda i: (i, 0))] * 3,
+    )(*outs)
     return tuple(a.reshape(latent.shape) for a in outs)
 
 

time: 137 us -> 134 us (0.978)
  local copies, waits for them, and re-layouts: 6.23 us -> 1.47 us
  Pallas kernels: 130 us -> 132 us
    unnamed x6 -> x1, local copies, waits for them, and re-layouts: 5.57 us -> 1.47 us
    pallas_call x0 -> x1, Pallas kernels: none -> 2.42 us  [shards(): pl.pallas_call(leave_kernel, grid=(2,), out_shape=[jax.ShapeDtypeStruct((...]
where the time goes in v5:
time: 134 us
  Pallas kernels  132 us (99%)
  local copies, waits for them, and re-layouts  1.47 us (1%)
    pallas_call x1, Pallas kernels, shards(): pl.pallas_call(functools.partial(kernel, nt, ns, batch), out_shape=[jax.S...  130 us

profile of v5, /device:TPU:1, one launch (start us, length us, event | category | flops | bytes accessed | tf_op | source)
XLA Modules:
  0.0 134.1 jit_solution(7952314609370621451)
XLA Ops:
  0.6 1.5 %copy.7.mod = f32[2,2,3,1152]{3,2,1,0:T(4,128)} copy(f32[2,2,3,1152]{3,1,2,0:T(2,128)} %param.6) | data formatting | bytes 110592 | tf_op args[2]
  2.1 129.6 %shard_map.67 = (bf16[256,1152]{1,0:T(8,128)(2,1)}, bf16[256,1152]{1,0:T(8,128)(2,1)}, bf16[256,1152]{1,0:T(8,128)(2,1)}) custom-call(bf16[256,1152]{1,0:T(8,128)(2,1)} %bitcast.11, bf16[256,1152]{1,0:T(8,128)(2,1)} %bitcast.12, f32[2,2,3,1152]{3,2,1,0:T(4,128)} %copy.7.mod, bf16[2,144,4608]{2,1,0:T(8,128)(2,1)} %weights.1), custom_call_target="tpu_custom_call" | custom-call | flops 6000000000 | bytes 20000000 | tf_op jit(solution)/shard_map/pallas_call | solution.py:411
  131.7 2.4 %shard_map.68 = (bf16[256,1152]{1,0:T(8,128)(2,1)}, bf16[256,1152]{1,0:T(8,128)(2,1)}, bf16[256,1152]{1,0:T(8,128)(2,1)}) custom-call(bf16[256,1152]{1,0:T(8,128)(2,1)} %get-tuple-element.9.refs_0_, bf16[256,1152]{1,0:T(8,128)(2,1)} %get-tuple-element.10.refs_1_, bf16[256,1152]{1,0:T(8,128)(2,1)} %get-tuple-element.11.refs_2_), custom_call_target="tpu_custom_call" | custom-call | tf_op jit(solution)/shard_map/pallas_call | solution.py:455

commit v6 on v5

--- a/solution.py
+++ b/solution.py
@@ -242,6 +242,7 @@
     tokens = Spread(x, send_x, recv_x, ns, t, s, [t] + [lax.rem(t + nt - k, nt) for k in range(1, nt)])
     tokens.begin(ready, 0, nt // 2)
     qkv_t.stage()
+    cols_t.stage()
     tokens.begin(ready, nt // 2, nt)
     qkv_t.stage()
     cols_t.stage()
@@ -279,8 +280,7 @@
         mine[p] = fold(jnp.concatenate(outs, axis=-1), 0, 1)
         pl.when(step < ns)(lambda: send_out(step, p).start())
         pl.when(step == 1)(cols_t.stage)
-        pl.when(step == 2)(cols_t.stage)
-        pl.when(step == 3)(lambda: (cols_t.stage(), cols_s.stage()) and None)
+        pl.when(step == 2)(lambda: (cols_t.stage(), cols_s.stage()) and None)
         return carry
 
     def collect():

time: 134 us -> 134 us (level)
  no operation moved by 1% of the time
where the time goes in v6:
time: 134 us
  Pallas kernels  132 us (99%)
  local copies, waits for them, and re-layouts  1.47 us (1%)
    pallas_call x1, Pallas kernels, shards(): pl.pallas_call(functools.partial(kernel, nt, ns, batch), out_shape=[jax.S...  130 us

profile of v6, /device:TPU:1, one launch (start us, length us, event | category | flops | bytes accessed | tf_op | source)
XLA Modules:
  0.0 134.3 jit_solution(2209168257131266775)
XLA Ops:
  0.6 1.5 %copy.7.mod = f32[2,2,3,1152]{3,2,1,0:T(4,128)} copy(f32[2,2,3,1152]{3,1,2,0:T(2,128)} %param.6) | data formatting | bytes 110592 | tf_op args[2]
  2.1 129.7 %shard_map.67 = (bf16[256,1152]{1,0:T(8,128)(2,1)}, bf16[256,1152]{1,0:T(8,128)(2,1)}, bf16[256,1152]{1,0:T(8,128)(2,1)}) custom-call(bf16[256,1152]{1,0:T(8,128)(2,1)} %bitcast.11, bf16[256,1152]{1,0:T(8,128)(2,1)} %bitcast.12, f32[2,2,3,1152]{3,2,1,0:T(4,128)} %copy.7.mod, bf16[2,144,4608]{2,1,0:T(8,128)(2,1)} %weights.1), custom_call_target="tpu_custom_call" | custom-call | flops 6000000000 | bytes 20000000 | tf_op jit(solution)/shard_map/pallas_call | solution.py:411
  131.8 2.4 %shard_map.68 = (bf16[256,1152]{1,0:T(8,128)(2,1)}, bf16[256,1152]{1,0:T(8,128)(2,1)}, bf16[256,1152]{1,0:T(8,128)(2,1)}) custom-call(bf16[256,1152]{1,0:T(8,128)(2,1)} %get-tuple-element.9.refs_0_, bf16[256,1152]{1,0:T(8,128)(2,1)} %get-tuple-element.10.refs_1_, bf16[256,1152]{1,0:T(8,128)(2,1)} %get-tuple-element.11.refs_2_), custom_call_target="tpu_custom_call" | custom-call | tf_op jit(solution)/shard_map/pallas_call | solution.py:455
